TPU v7x, 32 devices: a whole 2x2x4 slice. The times are simulated.
32 devices in a mesh: group: 2 (over x), mem: 16 (over z, y, core).
Axes of the slice: x: 2, y: 2, z: 4, core: 2. Of those that a mesh axis runs over, the one named last changes fastest.
Arguments:
- perturbations: bfloat16 [32, 256, 4, 1, 256], P(('group', 'mem')), parts along dimension 0, may hold values from -6 to 6
- gradient: bfloat16 [512, 4, 1, 256], P(('group', 'mem')), parts along dimension 0, may hold values from -6 to 6
Outputs:
- increment: bfloat16 [512, 4, 1, 256], P(('group', 'mem')), parts along dimension 0
There are 2 independent parts, one for each index of `group`. A program takes and returns all parts, laid end to end along the dimension named above; each array names one. Nothing has to cross between parts.
All inputs are finite; a program needn't handle non-finite values.
Results may differ from a plain program's by a relative error of at most 0.0085.
Values may be sent and summed in bfloat16 or wider, within the bound.
A program may use at most 64 MiB of HBM per device.

v0:
```python
import jax
import jax.numpy as jnp
from jax import lax
from jax.sharding import PartitionSpec as P

REACH = 8


def make_band(order):
    rows = jnp.arange(order, dtype=jnp.int32)
    offset = (rows[:, None] - rows[None, :]).astype(jnp.float32)
    weights = jnp.exp(-(offset * offset) / (4.0 * REACH))
    inside = jnp.abs(offset) <= REACH
    return jnp.where(inside, weights, jnp.float32(0.0)).astype(jnp.bfloat16)


def per_device(perturbations, gradient):
    local_rows, nvars, levels, columns = gradient.shape
    count_here = perturbations.shape[0]
    grid_rows = perturbations.shape[1]
    members = count_here * lax.axis_size("mem")
    band_x = make_band(columns)
    band_y = make_band(grid_rows)
    row_block = lax.all_to_all(perturbations, "mem", split_axis=1, concat_axis=0, tiled=True)
    mixed = jnp.sum(
        row_block.astype(jnp.float32) * gradient.astype(jnp.float32)[None], axis=2
    ).astype(jnp.bfloat16)
    along_x = jnp.dot(
        mixed.reshape(members * local_rows * levels, columns),
        band_x,
        preferred_element_type=jnp.float32,
    )
    along_x = along_x.astype(jnp.bfloat16).reshape(members, local_rows, levels, columns)
    whole_field = lax.all_to_all(along_x, "mem", split_axis=0, concat_axis=1, tiled=True)
    filtered = jnp.dot(
        band_y,
        whole_field.reshape(count_here, grid_rows, levels * columns)[0],
        preferred_element_type=jnp.float32,
    )
    filtered = filtered.astype(jnp.bfloat16).reshape(count_here, grid_rows, levels, columns)
    row_field = lax.all_to_all(filtered, "mem", split_axis=1, concat_axis=0, tiled=True)
    total = jnp.sum(
        row_block.astype(jnp.float32) * row_field.astype(jnp.float32)[:, :, None], axis=0
    )
    return (total * (1.0 / (members - 1))).astype(jnp.bfloat16)


def solution(mesh):
    in_specs = (P(("group", "mem"), None, None, None, None), P(("group", "mem"), None, None, None))
    out_specs = P(("group", "mem"), None, None, None)
    return jax.shard_map(
        per_device, mesh=mesh, in_specs=in_specs, out_specs=out_specs, check_vma=False
    )
```

profile of v0, /device:TPU:0, one launch (start us, length us, event | category | flops | bytes accessed | tf_op | source)
XLA Modules:
  0.0 49.1 jit_solution(8863171677678697585)
XLA Ops:
  0.0 0.0 copy-start
  0.0 7.5 %all-to-all-start = ((bf16[1,256,4,1,256]{4,2,3,0,1:T(4,128)(2,1)}), bf16[1,256,4,1,256]{4,2,3,0,1:T(4,128)(2,1)S(1)}, u32[]{:S(2)}, u32[]{:S(2)}) async-start(bf16[1,256,4,1,256]{4,2,3,0,1:T(4,128)(2,1)} %bitcast.27), calls=%async_computation | async-start | bytes 1048576 | tf_op jit(solution)/shard_map/all_to_all | solution.py:24
  7.5 0.0 copy-done
  7.6 14.4 %all-to-all-done = bf16[1,256,4,1,256]{4,2,3,0,1:T(4,128)(2,1)S(1)} async-done(((bf16[1,256,4,1,256]{4,2,3,0,1:T(4,128)(2,1)}), bf16[1,256,4,1,256]{4,2,3,0,1:T(4,128)(2,1)S(1)}, u32[]{:S(2)}, u32[]{:S(2)}) %all-to-all-start) | async-done | bytes 524320 | tf_op jit(solution)/shard_map/all_to_all | solution.py:24
  22.0 0.2 mul.62
  22.2 0.9 %multiply_reduce_fusion.1 = bf16[256,256]{1,0:T(8,128)(2,1)S(1)} fusion(f32[1,256,4,1,256]{4,2,3,0,1:T(4,128)S(1)} %bitcast.23, bf16[1,256,4,1,256]{4,2,3,0,1:T(4,128)(2,1)S(1)} %all-to-all-done), kind=kLoop, calls=%fused_computation.4 | loop fusion | flops 720896 | bytes 1703936 | tf_op jit(solution)/shard_map/reduce_sum | solution.py:25
  23.1 0.2 convolution_convert_fusion.1
  23.3 11.8 %all_to_all.12 = bf16[16,16,1,256]{3,1,2,0:T(8,128)(2,1)S(1)} all-to-all(bf16[16,16,1,256]{3,1,2,0:T(8,128)(2,1)S(1)} %bitcast.28), channel_id=1, replica_groups=mesh['group'=2,'mem'=16] {'mem'}, dimensions={0} | all-to-all | bytes 262144 | tf_op jit(solution)/shard_map/all_to_all | solution.py:34
  35.1 0.2 fusion
  35.4 0.2 copy.8
  35.6 0.5 %broadcast.44 = bf16[]{:T(256)} broadcast(bf16[]{:T(256)} %constant.20), dimensions={} | broadcast | bytes 4
  36.1 1.4 %reduce.3 = bf16[256,256]{1,0:T(8,128)(2,1)S(1)} reduce(bf16[256,1,1,256]{3,2,1,0:T(2,128)(2,1)S(1)} %bitcast.24, bf16[]{:T(256)} %broadcast.44), dimensions={1,2}, to_apply=%bitcast.21.reduce_sub_computation | reduce | bytes 262146
  37.5 10.5 %all_to_all.13 = bf16[16,2,2048]{2,1,0:T(2,128)(2,1)S(1)} all-to-all(bf16[16,2,2048]{2,1,0:T(2,128)(2,1)S(1)} %reshape.90), channel_id=1, replica_groups=mesh['group'=2,'mem'=16] {'mem'}, dimensions={0} | all-to-all | bytes 262144 | tf_op jit(solution)/shard_map/all_to_all | solution.py:41
  48.1 0.1 reshape.91
  48.2 0.3 multiply_reduce_fusion
  48.5 0.6 %fusion.2 = bf16[16,4,1,256]{3,1,2,0:T(4,128)(2,1)} fusion(f32[16,4,256]{2,1,0:T(4,128)S(1)} %multiply_reduce_fusion), kind=kLoop, calls=%fused_computation.9 | loop fusion | flops 32768 | bytes 98304 | tf_op jit(solution)/shard_map/convert_element_type | solution.py:45
  (3 shorter events, 0.1 us)
Async XLA Ops:
  0.0 7.5 %copy-start = (bf16[16,4,1,256]{3,1,2,0:T(4,128)(2,1)S(1)}, bf16[16,4,1,256]{3,1,2,0:T(4,128)(2,1)}, u32[]{:S(2)}) copy-start(bf16[16,4,1,256]{3,1,2,0:T(4,128)(2,1)} %param.3) | copy-start | bytes 98308
  0.0 22.0 %all-to-all-start = ((bf16[1,256,4,1,256]{4,2,3,0,1:T(4,128)(2,1)}), bf16[1,256,4,1,256]{4,2,3,0,1:T(4,128)(2,1)S(1)}, u32[]{:S(2)}, u32[]{:S(2)}) async-start(bf16[1,256,4,1,256]{4,2,3,0,1:T(4,128)(2,1)} %bitcast.27), calls=%async_computation | async-start | bytes 1048576 | tf_op jit(solution)/shard_map/all_to_all | solution.py:24
where the time goes:
time: 49.5 us; the launch traced here: 49.1 us
  blocking collectives  22.4 us (45%)
  waiting for transfers between devices  14.4 us (29%)
  starting transfers between devices  7.52 us (15%)
  other arithmetic  3.2 us (6%)
  local copies, waits for them, and re-layouts  1.09 us (2%)
    all_to_all x1, waiting for transfers between devices, per_device(): lax.all_to_all(perturbations, 'mem', split_axis=1, concat_axis=0, tiled=T...  14.4 us
    all_to_all x1, blocking collectives, per_device(): lax.all_to_all(along_x, 'mem', split_axis=0, concat_axis=1, tiled=True)  11.8 us
    all_to_all x1, blocking collectives, per_device(): lax.all_to_all(filtered, 'mem', split_axis=1, concat_axis=0, tiled=True)  10.5 us
    all_to_all x1, starting transfers between devices, per_device(): lax.all_to_all(perturbations, 'mem', split_axis=1, concat_axis=0, tiled=T...  7.52 us
    unnamed x1, other arithmetic  1.41 us
  transfers between devices with their start and end apart: 1, of which 1 were waited for; matrix products, arithmetic and copies ran while one was open for 0% of the time, Pallas kernels for 0%

commit v1 on v0

v1 whole, which is shorter than its diff:
```python
import functools

import jax
import jax.numpy as jnp
from jax import lax
from jax.experimental import pallas as pl
from jax.experimental.pallas import tpu as pltpu
from jax.sharding import PartitionSpec as P

REACH = 8
LANES = 128


def band_tile(order):
    rows = lax.broadcasted_iota(jnp.int32, (order, order), 0)
    cols = lax.broadcasted_iota(jnp.int32, (order, order), 1)
    offset = (rows - cols).astype(jnp.float32)
    weights = jnp.exp(-(offset * offset) / (4.0 * REACH))
    inside = jnp.abs(offset) <= REACH
    return jnp.where(inside, weights, jnp.float32(0.0)).astype(jnp.bfloat16)


def kernel(dims, pert_hbm, grad_ref, out_ref, pert, grads, prods, along, bandx, bandy, spread,
           own, pair_out, pair_in, row_out, row_in, far_out, far_in,
           load_sem, g1s, g1r, g2s, g2r, g3s, g3r, r1s, r1r, r2s, r2r, r3s, r3r):
    na, nb, nvars, tiles, local_rows = dims
    f32, bf16 = jnp.float32, jnp.bfloat16
    per = nvars * tiles
    size = local_rows * per
    group_rows = nb * 2 * local_rows
    me = lax.axis_index("mem")
    c = lax.rem(me, 2)
    b = lax.rem(me // 2, nb)
    a = me // (2 * nb)

    def at(a_, b_, c_):
        return (a_ * nb + b_) * 2 + c_

    def a_of(d):
        return lax.rem(a + d, na)

    def b_of(d):
        return lax.rem(b + d, nb)

    def remote(src, dst, send, recv, to):
        return pltpu.make_async_remote_copy(
            src_ref=src, dst_ref=dst, send_sem=send, recv_sem=recv,
            device_id={"mem": to}, device_id_type=pl.DeviceIdType.MESH)

    sibling = at(a, b, 1 - c)
    peers = [sibling] + [at(a_of(d), b, c) for d in range(1, na)] + [at(a, b_of(d), c) for d in range(1, nb)]
    load = pltpu.make_async_copy(pert_hbm, pert, load_sem)
    load.start()
    barrier = pltpu.get_barrier_semaphore()
    for peer in peers:
        pl.semaphore_signal(barrier, inc=1, device_id={"mem": peer}, device_id_type=pl.DeviceIdType.MESH)
    grads[me] = grad_ref[...]
    pl.semaphore_wait(barrier, len(peers))

    sends = []

    def send(copy):
        copy.start()
        sends.append(copy)

    def copy1(d):
        return remote(grads.at[me], grads.at[me], g1s.at[d], g1r.at[a], at(a_of(d), b, c))

    def copy2(da, db):
        block = grads.at[at(a_of(da), b, c)]
        return remote(block, block, g2s.at[da * nb + db], g2r.at[a_of(da) * nb + b], at(a, b_of(db), c))

    def copy3(da, db):
        j = a_of(da) * nb + b_of(db)
        block = grads.at[2 * j + c]
        return remote(block, block, g3s.at[j], g3r.at[j], sibling)

    a_order = sorted(range(1, na), key=lambda d: (-min(d, na - d), d))
    for d in a_order:
        send(copy1(d))
    for db in range(1, nb):
        send(copy2(0, db))
    send(copy3(0, 0))

    bandx[...] = band_tile(bandx.shape[0])
    bandy[...] = band_tile(bandy.shape[0])

    def multiply(j):
        rows = pl.ds(pl.multiple_of(j * size, size), size)
        prods[rows, :] = pert[rows, :].astype(f32) * grads[j].astype(f32)

    load.wait()
    multiply(me)
    nearest = sorted(range(1, na), key=lambda d: (min(d, na - d), d))
    for d in nearest:
        block = grads.at[at(a_of(d), b, c)]
        remote(block, block, g1s.at[0], g1r.at[a_of(d)], me).wait_recv()
        for db in range(1, nb):
            send(copy2(d, db))
        send(copy3(d, 0))
        multiply(at(a_of(d), b, c))
    for da in [0] + nearest:
        for db in range(1, nb):
            block = grads.at[at(a_of(da), b_of(db), c)]
            remote(block, block, g2s.at[0], g2r.at[a_of(da) * nb + b_of(db)], me).wait_recv()
            send(copy3(da, db))
            multiply(at(a_of(da), b_of(db), c))
        for db in range(nb):
            j = a_of(da) * nb + b_of(db)
            block = grads.at[2 * j + 1 - c]
            remote(block, block, g3s.at[0], g3r.at[j], me).wait_recv()
            multiply(2 * j + 1 - c)
        first = a_of(da) * group_rows
        halves = []
        for t in range(tiles):
            total = None
            for v in range(nvars):
                term = prods[pl.ds(first * per + t * nvars + v, group_rows, stride=per), :]
                total = term if total is None else total + term
            halves.append(total)
        mixed = jnp.concatenate(halves, axis=1).astype(bf16)
        rows = pl.ds(pl.multiple_of(first, group_rows), group_rows)
        along[rows, :] = jnp.dot(mixed, bandx[...], preferred_element_type=f32).astype(bf16)

    order = a_order + [0]

    def produce(d):
        group = a_of(d)
        rows = pl.ds(pl.multiple_of(group * group_rows, group_rows), group_rows)
        filtered = jnp.dot(bandy[rows, :], along[...], preferred_element_type=f32).astype(bf16).astype(f32)
        for t in range(tiles):
            for v in range(nvars):
                spread[pl.ds(t * nvars + v, group_rows, stride=per), :] = filtered[:, t * LANES:(t + 1) * LANES]

        def term(b_, c_):
            local = pl.ds(pl.multiple_of((b_ * 2 + c_) * size, size), size)
            whole = pl.ds(pl.multiple_of(at(group, b_, c_) * size, size), size)
            return spread[local, :] * pert[whole, :].astype(f32)

        for db in list(range(1, nb)) + [0]:
            j = group * nb + b_of(db)
            pair_out[j] = term(b_of(db), 1 - c).astype(bf16)
            send(remote(pair_out.at[j], pair_in.at[j], r1s.at[j], r1r.at[j], sibling))
        for db in range(nb):
            own[group * nb + b_of(db)] = term(b_of(db), c)

    def to_rows(d):
        group = a_of(d)
        for db in list(range(1, nb)) + [0]:
            j = group * nb + b_of(db)
            remote(pair_in.at[j], pair_in.at[j], r1s.at[0], r1r.at[j], me).wait_recv()
            total = own[j] + pair_in[j].astype(f32)
            if db == 0:
                own[j] = total
            else:
                row_out[j] = total.astype(bf16)
                send(remote(row_out.at[j], row_in.at[group * nb + b], r2s.at[j], r2r.at[group * nb + b],
                            at(a, b_of(db), c)))

    def to_far(d):
        group = a_of(d)
        total = own[group * nb + b]
        for db in range(1, nb):
            j = group * nb + b_of(db)
            remote(row_in.at[j], row_in.at[j], r2s.at[0], r2r.at[j], me).wait_recv()
            total = total + row_in[j].astype(f32)
        if d == 0:
            return total
        far_out[group] = total.astype(bf16)
        send(remote(far_out.at[group], far_in.at[a], r3s.at[group], r3r.at[a], at(group, b, c)))
        return None

    total = None
    for step in range(na + 2):
        if step < na:
            produce(order[step])
        if 0 <= step - 1 < na:
            to_rows(order[step - 1])
        if 0 <= step - 2 < na:
            total = to_far(order[step - 2])
    for d in nearest:
        j = a_of(d)
        remote(far_in.at[j], far_in.at[j], r3s.at[0], r3r.at[j], me).wait_recv()
        total = total + far_in[j].astype(f32)
    out_ref[...] = (total * (1.0 / (na * nb * 2 - 1))).astype(bf16)
    for copy in sends:
        copy.wait_send()


def flat(array):
    rows, nvars, columns = array.shape
    return array.reshape(rows, nvars, columns // LANES, LANES).transpose(0, 2, 1, 3).reshape(-1, LANES)


def per_device(perturbations, gradient):
    local_rows, nvars, levels, columns = gradient.shape
    grid_rows = perturbations.shape[1]
    count = lax.axis_size("mem")
    nb = 1
    while nb * nb * 4 <= count // 2:
        nb *= 2
    na = count // 2 // nb
    tiles = columns // LANES
    size = local_rows * nvars * tiles
    dma, bf16, f32 = pltpu.SemaphoreType.DMA, jnp.bfloat16, jnp.float32
    pairs = na * nb
    out = pl.pallas_call(
        functools.partial(kernel, (na, nb, nvars, tiles, local_rows)),
        out_shape=jax.ShapeDtypeStruct((size, LANES), bf16),
        in_specs=[pl.BlockSpec(memory_space=pl.ANY), pl.BlockSpec(memory_space=pltpu.VMEM)],
        out_specs=pl.BlockSpec(memory_space=pltpu.VMEM),
        scratch_shapes=[
            pltpu.VMEM((count * size, LANES), bf16),
            pltpu.VMEM((count, size, LANES), bf16),
            pltpu.VMEM((count * size, LANES), f32),
            pltpu.VMEM((grid_rows, columns), bf16),
            pltpu.VMEM((columns, columns), bf16),
            pltpu.VMEM((grid_rows, grid_rows), bf16),
            pltpu.VMEM((nb * 2 * size, LANES), f32),
            pltpu.VMEM((pairs, size, LANES), f32),
            pltpu.VMEM((pairs, size, LANES), bf16),
            pltpu.VMEM((pairs, size, LANES), bf16),
            pltpu.VMEM((pairs, size, LANES), bf16),
            pltpu.VMEM((pairs, size, LANES), bf16),
            pltpu.VMEM((na, size, LANES), bf16),
            pltpu.VMEM((na, size, LANES), bf16),
            dma,
            dma((na,)), dma((na,)),
            dma((pairs,)), dma((pairs,)),
            dma((pairs,)), dma((pairs,)),
            dma((pairs,)), dma((pairs,)),
            dma((pairs,)), dma((pairs,)),
            dma((na,)), dma((na,)),
        ],
        compiler_params=pltpu.CompilerParams(
            collective_id=0, has_side_effects=True, vmem_limit_bytes=60 * 2**20),
    )(flat(perturbations.reshape(grid_rows, nvars, columns)), flat(gradient.reshape(local_rows, nvars, columns)))
    out = out.reshape(local_rows, tiles, nvars, LANES).transpose(0, 2, 1, 3)
    return out.reshape(local_rows, nvars, levels, columns)


def solution(mesh):
    in_specs = (P(("group", "mem"), None, None, None, None), P(("group", "mem"), None, None, None))
    out_specs = P(("group", "mem"), None, None, None)
    return jax.shard_map(
        per_device, mesh=mesh, in_specs=in_specs, out_specs=out_specs, check_vma=False
    )
```

time: 49.5 us -> 29.1 us (0.59)
  Pallas kernels: 0 us -> 27.4 us
  blocking collectives: 22.4 us -> 0 us
  waiting for transfers between devices: 14.4 us -> 0 us
  starting transfers between devices: 7.52 us -> 0 us
  other arithmetic: 3.2 us -> 0 us
    pallas_call x0 -> x1, Pallas kernels: none -> 27.4 us  [per_device(): pl.pallas_call(functools.partial(kernel, (na, nb, nvars, tiles, local_row...]
    all_to_all x2 -> x0, blocking collectives: 22.4 us -> none  [the longest x1 11.8 us: per_device(): lax.all_to_all(along_x, 'mem', split_axis=0, concat_axis=1, tiled=True)]
    all_to_all x1 -> x0, waiting for transfers between devices: 14.4 us -> none  [per_device(): lax.all_to_all(perturbations, 'mem', split_axis=1, concat_axis=0, tiled=T...]
    all_to_all x1 -> x0, starting transfers between devices: 7.52 us -> none  [per_device(): lax.all_to_all(perturbations, 'mem', split_axis=1, concat_axis=0, tiled=T...]
    unnamed x1 -> x0, other arithmetic: 1.41 us -> none
    reduce_sum x2 -> x0, other arithmetic: 1.15 us -> none  [the longest x1 0.86 us: per_device(): jnp.sum(row_block.astype(jnp.float32) * gradient.astype(jnp.float32)[None...]
    unnamed x6 -> x1, local copies, waits for them, and re-layouts: 0.7 us -> 1.39 us
    convert_element_type x1 -> x0, other arithmetic: 0.63 us -> none  [per_device(): return (total * (1.0 / (members - 1))).astype(jnp.bfloat16)]
  transfers between devices with their start and end apart: 1 -> 0, of which waited for: 1 -> 0; matrix products, arithmetic and copies ran while one was open for 0% -> 0% of each run, Pallas kernels for 0% -> 0%
where the time goes in v1:
time: 29.1 us; the launch traced here: 28.8 us
  Pallas kernels  27.4 us (94%)
  local copies, waits for them, and re-layouts  1.39 us (5%)
    pallas_call x1, Pallas kernels, per_device(): pl.pallas_call(functools.partial(kernel, (na, nb, nvars, tiles, local_row...  27.4 us
    unnamed x1, local copies, waits for them, and re-layouts  1.39 us

profile of v1, /device:TPU:0, one launch (start us, length us, event | category | flops | bytes accessed | tf_op | source)
XLA Modules:
  0.0 28.8 jit_solution(16646822271489135086)
XLA Ops:
  0.0 27.4 %shard_map.28 = bf16[128,128]{1,0:T(8,128)(2,1)} custom-call(bf16[2048,128]{1,0:T(8,128)(2,1)} %bitcast.15, bf16[128,128]{1,0:T(8,128)(2,1)} %bitcast.17), custom_call_target="tpu_custom_call" | custom-call | tf_op jit(solution)/shard_map/pallas_call | solution.py:207
  27.4 1.4 %copy.7 = bf16[16,4,1,256]{3,1,2,0:T(4,128)(2,1)} copy(bf16[16,4,1,256]{3,1,2,0:T(4,128)(2,1)} %bitcast.16) | data formatting | bytes 65536

commit v2 on v1

v2 whole, which is shorter than its diff:
```python
import functools

import jax
import jax.numpy as jnp
from jax import lax
from jax.experimental import pallas as pl
from jax.experimental.pallas import tpu as pltpu
from jax.sharding import PartitionSpec as P

REACH = 8
LANES = 128


def band_tile(order):
    rows = lax.broadcasted_iota(jnp.int32, (order, order), 0)
    cols = lax.broadcasted_iota(jnp.int32, (order, order), 1)
    offset = (rows - cols).astype(jnp.float32)
    weights = jnp.exp(-(offset * offset) / (4.0 * REACH))
    inside = jnp.abs(offset) <= REACH
    return jnp.where(inside, weights, jnp.float32(0.0)).astype(jnp.bfloat16)


def kernel(dims, pert_hbm, grad_hbm, out_ref, pert, grads, prods, along, bandx, bandy, spread,
           own, pair_out, pair_in, far_out, far_in,
           load_sem, grad_sem, g1s, g1r, g2s, g2r, r1s, r1r, r2s, r2r):
    na, nb, nvars, tiles, local_rows = dims
    f32, bf16 = jnp.float32, jnp.bfloat16
    per = nvars * tiles
    size = local_rows * per
    group_rows = nb * 2 * local_rows
    me = lax.axis_index("mem")
    c = lax.rem(me, 2)
    b = lax.rem(me // 2, nb)
    a = me // (2 * nb)

    def at(a_, b_, c_):
        return (a_ * nb + b_) * 2 + c_

    def a_of(d):
        return lax.rem(a + d, na)

    def b_of(d):
        return lax.rem(b + d, nb)

    def remote(src, dst, send, recv, to):
        return pltpu.make_async_remote_copy(
            src_ref=src, dst_ref=dst, send_sem=send, recv_sem=recv,
            device_id={"mem": to}, device_id_type=pl.DeviceIdType.MESH)

    def arrived(ref, send, recv):
        remote(ref, ref, send, recv, sibling).wait_recv()

    sibling = at(a, b, 1 - c)
    near = sorted(range(na), key=lambda d: (min(d, na - d), d))
    far = near[::-1]
    chips = [(da, db) for da in far for db in list(range(1, nb)) + [0] if da or db]
    peers = [at(a_of(da), b_of(db), c) for da, db in chips] + [sibling]
    barrier = pltpu.get_barrier_semaphore()
    for peer in peers:
        pl.semaphore_signal(barrier, inc=1, device_id={"mem": peer}, device_id_type=pl.DeviceIdType.MESH)
    mine = grads.at[c, a, b]
    grad_load = pltpu.make_async_copy(grad_hbm, mine, grad_sem)
    grad_load.start()
    load = pltpu.make_async_copy(pert_hbm, pert, load_sem)
    load.start()
    grad_load.wait()
    pl.semaphore_wait(barrier, len(peers))

    sends = []

    def send(copy):
        copy.start()
        sends.append(copy)

    for da, db in chips:
        send(remote(mine, mine, g1s.at[da * nb + db], g1r.at[a * nb + b], at(a_of(da), b_of(db), c)))

    bandx[...] = band_tile(bandx.shape[0])
    bandy[...] = band_tile(bandy.shape[0])

    def multiply(a_, b_, c_):
        rows = pl.ds(pl.multiple_of(at(a_, b_, c_) * size, size), size)
        prods[rows, :] = pert[rows, :].astype(f32) * grads[c_, a_, b_].astype(f32)

    load.wait()
    for da in near:
        group = a_of(da)
        for db in range(nb):
            if da or db:
                arrived(grads.at[c, group, b_of(db)], g1s.at[0], g1r.at[group * nb + b_of(db)])
        block = grads.at[c, group]
        send(remote(block, block, g2s.at[group], g2r.at[group], sibling))
        for db in range(nb):
            multiply(group, b_of(db), c)
    for da in near:
        group = a_of(da)
        arrived(grads.at[1 - c, group], g2s.at[0], g2r.at[group])
        for db in range(nb):
            multiply(group, db, 1 - c)
        first = group * group_rows
        halves = []
        for t in range(tiles):
            total = None
            for v in range(nvars):
                term = prods[pl.ds(first * per + t * nvars + v, group_rows, stride=per), :]
                total = term if total is None else total + term
            halves.append(total)
        mixed = jnp.concatenate(halves, axis=1).astype(bf16)
        rows = pl.ds(pl.multiple_of(first, group_rows), group_rows)
        along[rows, :] = jnp.dot(mixed, bandx[...], preferred_element_type=f32).astype(bf16)

    def produce(d):
        group = a_of(d)
        rows = pl.ds(pl.multiple_of(group * group_rows, group_rows), group_rows)
        filtered = jnp.dot(bandy[rows, :], along[...], preferred_element_type=f32).astype(bf16).astype(f32)
        for t in range(tiles):
            for v in range(nvars):
                spread[pl.ds(t * nvars + v, group_rows, stride=per), :] = filtered[:, t * LANES:(t + 1) * LANES]

        def term(b_, c_):
            local = pl.ds(pl.multiple_of((b_ * 2 + c_) * size, size), size)
            whole = pl.ds(pl.multiple_of(at(group, b_, c_) * size, size), size)
            return spread[local, :] * pert[whole, :].astype(f32)

        for b_ in range(nb):
            pair_out[group, b_] = term(b_, 1 - c).astype(bf16)
        send(remote(pair_out.at[group], pair_in.at[group], r1s.at[group], r1r.at[group], sibling))
        for b_ in range(nb):
            own[group, b_] = term(b_, c)

    def forward(d):
        group = a_of(d)
        arrived(pair_in.at[group], r1s.at[0], r1r.at[group])
        for db in list(range(1, nb)) + [0]:
            b_ = b_of(db)
            total = own[group, b_] + pair_in[group, b_].astype(f32)
            if d == 0 and db == 0:
                return total
            j = group * nb + b_
            far_out[j] = total.astype(bf16)
            send(remote(far_out.at[j], far_in.at[a * nb + b], r2s.at[j], r2r.at[a * nb + b], at(group, b_, c)))
        return None

    total = None
    for step in range(na + 1):
        if step < na:
            produce(far[step])
        if step:
            total = forward(far[step - 1])
    for da, db in chips[::-1]:
        j = a_of(da) * nb + b_of(db)
        arrived(far_in.at[j], r2s.at[0], r2r.at[j])
        total = total + far_in[j].astype(f32)
    out_ref[...] = (total * (1.0 / (na * nb * 2 - 1))).astype(bf16)
    for copy in sends:
        copy.wait_send()


def flat(array):
    rows, nvars, columns = array.shape
    return array.reshape(rows, nvars, columns // LANES, LANES).transpose(0, 2, 1, 3).reshape(-1, LANES)


def per_device(perturbations, gradient):
    local_rows, nvars, levels, columns = gradient.shape
    grid_rows = perturbations.shape[1]
    count = lax.axis_size("mem")
    nb = 1
    while nb * nb * 4 <= count // 2:
        nb *= 2
    na = count // 2 // nb
    tiles = columns // LANES
    size = local_rows * nvars * tiles
    dma, bf16, f32 = pltpu.SemaphoreType.DMA, jnp.bfloat16, jnp.float32
    pairs = na * nb
    out = pl.pallas_call(
        functools.partial(kernel, (na, nb, nvars, tiles, local_rows)),
        out_shape=jax.ShapeDtypeStruct((size, LANES), bf16),
        in_specs=[pl.BlockSpec(memory_space=pltpu.HBM)] * 2,
        out_specs=pl.BlockSpec(memory_space=pltpu.VMEM),
        scratch_shapes=[
            pltpu.VMEM((count * size, LANES), bf16),
            pltpu.VMEM((2, na, nb, size, LANES), bf16),
            pltpu.VMEM((count * size, LANES), f32),
            pltpu.VMEM((grid_rows, columns), bf16),
            pltpu.VMEM((columns, columns), bf16),
            pltpu.VMEM((grid_rows, grid_rows), bf16),
            pltpu.VMEM((nb * 2 * size, LANES), f32),
            pltpu.VMEM((na, nb, size, LANES), f32),
            pltpu.VMEM((na, nb, size, LANES), bf16),
            pltpu.VMEM((na, nb, size, LANES), bf16),
            pltpu.VMEM((pairs, size, LANES), bf16),
            pltpu.VMEM((pairs, size, LANES), bf16),
            dma, dma,
            dma((pairs,)), dma((pairs,)),
            dma((na,)), dma((na,)),
            dma((na,)), dma((na,)),
            dma((pairs,)), dma((pairs,)),
        ],
        compiler_params=pltpu.CompilerParams(
            collective_id=0, has_side_effects=True, vmem_limit_bytes=60 * 2**20),
    )(flat(perturbations.reshape(grid_rows, nvars, columns)), flat(gradient.reshape(local_rows, nvars, columns)))
    out = out.reshape(local_rows, tiles, nvars, LANES).transpose(0, 2, 1, 3)
    return out.reshape(local_rows, nvars, levels, columns)


def solution(mesh):
    in_specs = (P(("group", "mem"), None, None, None, None), P(("group", "mem"), None, None, None))
    out_specs = P(("group", "mem"), None, None, None)
    return jax.shard_map(
        per_device, mesh=mesh, in_specs=in_specs, out_specs=out_specs, check_vma=False
    )
```

time: 29.1 us -> 24.4 us (0.84)
  Pallas kernels: 27.4 us -> 22.8 us
    pallas_call x1, Pallas kernels: 27.4 us -> 22.8 us  [per_device(): pl.pallas_call(functools.partial(kernel, (na, nb, nvars, tiles, local_row...]
where the time goes in v2:
time: 24.4 us; the launch traced here: 24.2 us
  Pallas kernels  22.8 us (93%)
  local copies, waits for them, and re-layouts  1.39 us (6%)
    pallas_call x1, Pallas kernels, per_device(): pl.pallas_call(functools.partial(kernel, (na, nb, nvars, tiles, local_row...  22.8 us
    unnamed x1, local copies, waits for them, and re-layouts  1.39 us

profile of v2, /device:TPU:0, one launch (start us, length us, event | category | flops | bytes accessed | tf_op | source)
XLA Modules:
  0.0 24.2 jit_solution(4263113426008608578)
XLA Ops:
  0.0 22.8 %shard_map.28 = bf16[128,128]{1,0:T(8,128)(2,1)} custom-call(bf16[2048,128]{1,0:T(8,128)(2,1)} %bitcast.15, bf16[128,128]{1,0:T(8,128)(2,1)} %bitcast.17), custom_call_target="tpu_custom_call" | custom-call | tf_op jit(solution)/shard_map/pallas_call | solution.py:176
  22.8 1.4 %copy.7 = bf16[16,4,1,256]{3,1,2,0:T(4,128)(2,1)} copy(bf16[16,4,1,256]{3,1,2,0:T(4,128)(2,1)} %bitcast.16) | data formatting | bytes 65536

commit v3 on v2

--- a/solution.py
+++ b/solution.py
@@ -198,7 +198,7 @@
             dma((pairs,)), dma((pairs,)),
         ],
         compiler_params=pltpu.CompilerParams(
-            collective_id=0, has_side_effects=True, vmem_limit_bytes=60 * 2**20),
+            collective_id=0, has_side_effects=True, vmem_limit_bytes=56518246),
     )(flat(perturbations.reshape(grid_rows, nvars, columns)), flat(gradient.reshape(local_rows, nvars, columns)))
     out = out.reshape(local_rows, tiles, nvars, LANES).transpose(0, 2, 1, 3)
     return out.reshape(local_rows, nvars, levels, columns)

time: 24.4 us -> 23 us (0.943)
  local copies, waits for them, and re-layouts: 1.39 us -> 0.62 us
  Pallas kernels: 22.8 us -> 22.2 us
    unnamed x1, local copies, waits for them, and re-layouts: 1.39 us -> 0.62 us
    pallas_call x1, Pallas kernels: 22.8 us -> 22.2 us  [per_device(): pl.pallas_call(functools.partial(kernel, (na, nb, nvars, tiles, local_row...]
where the time goes in v3:
time: 23 us; the launch traced here: 22.8 us
  Pallas kernels  22.2 us (97%)
  local copies, waits for them, and re-layouts  0.62 us (3%)
    pallas_call x1, Pallas kernels, per_device(): pl.pallas_call(functools.partial(kernel, (na, nb, nvars, tiles, local_row...  22.2 us
    unnamed x1, local copies, waits for them, and re-layouts  0.62 us

profile of v3, /device:TPU:0, one launch (start us, length us, event | category | flops | bytes accessed | tf_op | source)
XLA Modules:
  0.0 22.8 jit_solution(13284755755064379557)
XLA Ops:
  0.0 22.2 %shard_map.28 = bf16[128,128]{1,0:T(8,128)(2,1)S(1)} custom-call(bf16[2048,128]{1,0:T(8,128)(2,1)} %bitcast.16, bf16[128,128]{1,0:T(8,128)(2,1)} %bitcast.17), custom_call_target="tpu_custom_call" | custom-call | tf_op jit(solution)/shard_map/pallas_call | solution.py:176
  22.2 0.6 %copy.7 = bf16[16,4,1,256]{3,1,2,0:T(4,128)(2,1)} copy(bf16[16,4,1,256]{3,1,2,0:T(4,128)(2,1)S(1)} %bitcast.15) | data formatting | bytes 65536
